TPU v7x, 32 devices: a whole 2x2x4 slice. The times are simulated.
32 devices in a mesh: step: 4 (over y, x), seq: 8 (over z, core).
Axes of the slice: x: 2, y: 2, z: 4, core: 2. Of those that a mesh axis runs over, the one named last changes fastest.
Arguments:
- latents: float32 [4, 256, 64], P('step', 'seq'), may hold values from -6 to 6
- timesteps: int32 [5], replicated, may hold values from 0 to 1000, as said below
- embed_weight: bfloat16 [64, 4096], replicated, may hold values from -0.75 to 0.75
- mod_weight: float32 [256, 2, 4096], P('seq'), may hold values from -0.375 to 0.375
- qkv_weight: bfloat16 [4096, 8, 3, 128], P('step', 'seq'), may hold values from -0.09375 to 0.09375
- out_weight: bfloat16 [8, 128, 64], P('seq'), may hold values from -6 to 6
Outputs:
- updated: float32 [4, 256, 64], P('step', 'seq')
- velocity: float32 [4, 256, 64], P('step', 'seq')
Inputs may be any that keep to these rules, and one draw needn't show every extreme that they name: `timesteps`: strictly decreasing along the table.
All inputs are finite; a program needn't handle non-finite values.
Results may differ from a plain program's by a relative error of at most 0.0049.
Values may be sent and summed in bfloat16 or wider, within the bound.
A program may use at most 64 MiB of HBM per device.

v0:
```python
import math

import jax
import jax.numpy as jnp
from jax import lax
from jax.sharding import PartitionSpec as P

FREQ = 256


def carried_in(shard, axis, combine, identity):
    devices, place = (lax.axis_size(axis), lax.axis_index(axis))
    everything = lax.all_gather(shard, axis)
    start = jnp.broadcast_to(jnp.asarray(identity, shard.dtype), shard.shape)

    def step(k, before):
        reached = k < place
        new = combine(before, everything[k])
        return jnp.where(reached, new, before)

    return lax.fori_loop(0, devices, step, start)


def condition_of(stamp):
    half_count = FREQ // 2
    frequencies = jnp.exp(
        -math.log(10000.0) * jnp.arange(half_count, dtype=jnp.float32) / half_count
    )
    angles = stamp * frequencies
    return jnp.concatenate([jnp.cos(angles), jnp.sin(angles)])


def modulate(latent_rows, embed_weight, shift_vec, scale_vec):
    embedded = jnp.dot(latent_rows, embed_weight, preferred_element_type=jnp.float32)
    center_mean = jnp.mean(embedded, axis=-1, keepdims=True)
    centered = embedded - center_mean
    variance = jnp.mean(centered * centered, axis=-1, keepdims=True)
    normed = centered * lax.rsqrt(variance + 1e-06)
    return (normed * (1.0 + scale_vec) + shift_vec).astype(jnp.bfloat16)


def qk_norm(head_rows):
    as_float = head_rows.astype(jnp.float32)
    return (
        as_float * lax.rsqrt(jnp.mean(as_float * as_float, axis=-1, keepdims=True) + 1e-06)
    ).astype(jnp.bfloat16)


def attend_head(head_block):
    queries = qk_norm(head_block[:, 0])
    key_rows = qk_norm(head_block[:, 1])
    values = head_block[:, 2]
    seq_length = queries.shape[0]
    head_dim = queries.shape[1]
    block_rows = math.gcd(seq_length, 512)
    query_blocks = queries.reshape(seq_length // block_rows, block_rows, head_dim)

    def one_block(query_block):
        scores = jnp.dot(query_block, key_rows.T, preferred_element_type=jnp.float32) * (
            1.0 / math.sqrt(head_dim)
        )
        weights = jnp.exp(scores)
        probabilities = (weights / jnp.sum(weights, axis=-1, keepdims=True)).astype(jnp.bfloat16)
        return jnp.dot(probabilities, values, preferred_element_type=jnp.float32).astype(
            jnp.bfloat16
        )

    return lax.map(one_block, query_blocks).reshape(seq_length, head_dim)


def add_terms(earlier_sum, later_sum):
    return earlier_sum + later_sum


def on_device(latents, timesteps, embed_weight, mod_weight, qkv_weight, out_weight):
    step_index = lax.axis_index("step")
    seq_index = lax.axis_index("seq")
    stamp_pair = lax.dynamic_slice_in_dim(timesteps, step_index, 2, 0).astype(jnp.float32)
    condition_vec = condition_of(stamp_pair[0])
    feature_rows = mod_weight.shape[0]
    local_features = lax.dynamic_slice_in_dim(
        condition_vec, seq_index * feature_rows, feature_rows, 0
    )
    partial_mod = jnp.einsum(
        "f,fcd->cd", local_features, mod_weight, precision=lax.Precision.HIGHEST
    )
    modulation = lax.psum(partial_mod, "seq")
    own_latents = latents[0].astype(jnp.bfloat16)
    all_latents = lax.all_gather(own_latents, "seq", axis=0, tiled=True)
    gathered = modulate(all_latents, embed_weight, modulation[0], modulation[1])
    seq_length = gathered.shape[0]
    heads_here = qkv_weight.shape[1]
    head_dim = qkv_weight.shape[3]
    qkv_width = heads_here * 3 * head_dim
    weight_piece = lax.all_gather(qkv_weight, "step", axis=0, tiled=True)
    flat_piece = weight_piece.reshape(weight_piece.shape[0], qkv_width)
    accumulated = jnp.dot(gathered, flat_piece, preferred_element_type=jnp.float32)
    projected = accumulated.astype(jnp.bfloat16).reshape(seq_length, heads_here, 3, head_dim)
    attended = lax.map(attend_head, jnp.moveaxis(projected, 1, 0))
    merged_heads = jnp.moveaxis(attended, 0, 1).reshape(seq_length, heads_here * head_dim)
    out_matrix = out_weight.reshape(heads_here * head_dim, out_weight.shape[2])
    velocity = lax.psum_scatter(
        jnp.dot(merged_heads, out_matrix, preferred_element_type=jnp.float32),
        "seq",
        scatter_dimension=0,
        tiled=True,
    )
    step_size = (stamp_pair[1] - stamp_pair[0]) / 1000.0
    increment = step_size * velocity + jnp.where(
        step_index == 0, latents[0], jnp.zeros_like(latents[0])
    )
    earlier = carried_in(increment, "step", add_terms, jnp.zeros_like(increment))
    updated = earlier + increment
    return (updated[None], velocity[None])


def solution(mesh):
    in_specs = (
        P("step", "seq", None),
        P(),
        P(),
        P("seq", None, None),
        P("step", "seq", None, None),
        P("seq", None, None),
    )
    out_specs = (P("step", "seq", None), P("step", "seq", None))
    return jax.shard_map(
        on_device, mesh=mesh, in_specs=in_specs, out_specs=out_specs, check_vma=False
    )
```

profile of v0, /device:TPU:0, one launch (start us, length us, event | category | flops | bytes accessed | tf_op | source)
XLA Modules:
  0.0 113.8 jit_solution(4033060275992303720)
XLA Ops:
  7.2 0.0 copy-start
  7.2 0.0 all-gather.4.cloned.1.call-start
  7.2 2.4 %copy.8 = bf16[1024,1,3,128]{0,3,2,1:T(8,128)(2,1)} copy(bf16[1024,1,3,128]{3,0,2,1:T(8,128)(2,1)} %param.12) | data formatting | bytes 1572864 | tf_op args[4]
  9.6 0.0 all-gather.4.cloned.1.call-update
  9.6 0.0 reduce-scatter.2.cloned.1.call-start
  9.7 0.7 convert_element_type.52
  10.4 0.7 dynamic-slice_convert_fusion
  11.1 0.6 fusion.31
  11.7 0.7 fusion.29
  12.4 0.0 copy-done
  12.5 1.2 %fusion.8 = f32[1,2,4096]{2,0,1:T(1,128)S(1)} fusion(f32[32,2,4096]{2,1,0:T(2,128)S(1)} %copy-done, f32[256]{0:T(256)S(1)} %pad_maximum_fusion, s32[]{:T(128)S(6)} %select_n.37), kind=kOutput, calls=%fused_computation.13 | convolution fusion | flops 3145728 | bytes 1081860 | tf_op jit(solution)/shard_map/f,fcd->cd/dot_general | solution.py:84
  13.7 15.7 %all-gather = bf16[1,256,64]{2,1,0:T(8,128)(2,1)S(1)} all-gather(bf16[1,32,64]{2,1,0:T(8,128)(2,1)S(1)} %convert_element_type.52), channel_id=2, replica_groups=mesh['step'=4,'seq'=8] {'seq'}, dimensions={1}, use_global_device_ids=true | all-gather | bytes 36864 | tf_op jit(solution)/shard_map/all_gather | solution.py:89
  29.3 29.1 %psum.7 = f32[2,4096]{1,0:T(2,128)S(1)} all-reduce(f32[2,4096]{1,0:T(2,128)S(1)} %bitcast.53), channel_id=1, replica_groups=mesh['step'=4,'seq'=8] {'seq'}, use_global_device_ids=true, to_apply=%region_2.0 | all-reduce | flops 8192 | bytes 65536 | tf_op jit(solution)/shard_map/psum | solution.py:87
  58.4 1.8 %fusion.32 = (f32[256]{0:T(256)S(1)}, f32[256,4096]{1,0:T(8,128)S(1)}) fusion(bf16[64,4096]{1,0:T(8,128)(2,1)} %param.10, bf16[1,256,64]{2,1,0:T(8,128)(2,1)S(1)} %all-gather), kind=kOutput, calls=%fused_computation.51 | convolution fusion | flops 135266048 | bytes 4752384 | tf_op jit(solution)/shard_map/dot_general | solution.py:34
  60.2 0.0 copy-start.1
  60.2 1.9 %copy-done.1 = f32[256,4096]{1,0:T(8,128)} copy-done((f32[256,4096]{1,0:T(8,128)}, f32[256,4096]{1,0:T(8,128)S(1)}, u32[]{:S(2)}) %copy-start.1) | copy-done | bytes 4194328
  62.1 0.6 multiply_reduce_fusion
  62.7 0.0 all-gather.4.cloned.1.call-done
  62.8 0.0 copy-start.3
  62.8 0.0 copy-start.2
  62.8 4.5 %fusion.5 = bf16[256,384]{1,0:T(8,128)(2,1)S(1)} fusion(bf16[4096,384]{0,1:T(8,128)(2,1)} %bitcast.57, f32[256,4096]{1,0:T(8,128)} %copy-done.1, f32[4096]{0:T(1024)S(1)} %bitcast.56, f32[4096]{0:T(1024)S(1)} %bitcast.55, f32[256]{0:T(256)S(1)} %add_rsqrt_fusion.2, f32[256]{0:T(256)S(1)} %broadcast_multiply_fusion), kind=kOutput, calls=%fused_computation.8 | convolution fusion | flops 810647552 | bytes 7571456 | tf_op jit(solution)/shard_map/dot_general | solution.py:97
  67.3 0.1 copy.9
  67.5 0.3 fusion.33
  67.8 0.0 copy-done.3
  67.8 1.0 fusion.7
  68.8 0.0 reduce-scatter.2.cloned.1.call-update
  70.1 27.3 %reduce-scatter.2.cloned.1.call-done = f32[32,64]{1,0:T(8,128)} async-done(((f32[256,64]{1,0:T(8,128)}), f32[32,64]{1,0:T(8,128)}) %reduce-scatter.2.cloned.1.call-update) | async-done | bytes 8208 | tf_op jit(solution)/shard_map/reduce_scatter | solution.py:102
  97.3 0.0 copy-done.2
  97.3 0.7 bitcast_add_fusion
  98.1 8.2 %all-gather.1 = f32[128,64]{1,0:T(8,128)S(1)} all-gather(f32[32,64]{1,0:T(8,128)S(1)} %bitcast_add_fusion), channel_id=3, replica_groups=mesh['step'=4,'seq'=8] {'step'}, dimensions={0}, use_global_device_ids=true | all-gather | bytes 40960 | tf_op jit(solution)/shard_map/all_gather | solution.py:13
  106.2 0.1 while.15
  106.4 0.6 add_bitcast_fusion
  (13 shorter events, 0.2 us)
Async XLA Ops:
  7.2 5.3 %copy-start = (f32[32,2,4096]{2,1,0:T(2,128)S(1)}, f32[32,2,4096]{2,1,0:T(2,128)}, u32[]{:S(2)}) copy-start(f32[32,2,4096]{2,1,0:T(2,128)} %param.11) | copy-start | bytes 3145732
  7.2 55.6 %all-gather.4.cloned.1.call-start = ((), (), s32[]{:S(2)}) async-start(), calls=%async_computation.1 | async-start | bytes 3932160 | tf_op jit(solution)/shard_map/all_gather | solution.py:95
  9.6 87.7 %reduce-scatter.2.cloned.1.call-start = ((), (), s32[]{:S(2)}) async-start(), calls=%async_computation.2 | async-start | bytes 147456 | tf_op jit(solution)/shard_map/reduce_scatter | solution.py:102
  60.2 1.9 %copy-start.1 = (f32[256,4096]{1,0:T(8,128)}, f32[256,4096]{1,0:T(8,128)S(1)}, u32[]{:S(2)}) copy-start(f32[256,4096]{1,0:T(8,128)S(1)} %get-tuple-element.141) | copy-start | bytes 12582916
  62.8 5.0 %copy-start.3 = (bf16[1,128,64]{1,2,0:T(8,128)(2,1)S(1)}, bf16[1,128,64]{1,2,0:T(8,128)(2,1)}, u32[]{:S(2)}) copy-start(bf16[1,128,64]{1,2,0:T(8,128)(2,1)} %param.13) | copy-start | bytes 49156
  62.8 34.6 %copy-start.2 = (f32[1,32,64]{2,1,0:T(8,128)S(1)}, f32[1,32,64]{2,1,0:T(8,128)}, u32[]{:S(2)}) copy-start(f32[1,32,64]{2,1,0:T(8,128)} %param.8) | copy-start | bytes 24580
Sparse Core Ops, SparseCore 0:
  9.9 46.7 all-gather.3
  68.9 28.3 reduce-scatter.1
where the time goes:
time: 114 us
  blocking collectives  52.9 us (46%)
  waiting for transfers between devices  27.3 us (24%)
  between operations  15.4 us (14%)
  matrix products  8.72 us (8%)
  local copies, waits for them, and re-layouts  5.06 us (4%)
  other arithmetic  4.22 us (4%)
    psum x1, blocking collectives, on_device(): modulation = lax.psum(partial_mod, 'seq')  29.1 us
    reduce_scatter x1, waiting for transfers between devices, on_device(): lax.psum_scatter(jnp.dot(merged_heads, out_matrix, preferred_element_type...  27.3 us
    all_gather x1, blocking collectives, on_device(): all_latents = lax.all_gather(own_latents, 'seq', axis=0, tiled=True)  15.7 us
    all_gather x1, blocking collectives, carried_in(): everything = lax.all_gather(shard, axis)  8.18 us
    dot_general x1, matrix products, on_device(): jnp.dot(gathered, flat_piece, preferred_element_type=jnp.float32)  4.48 us
    unnamed x9, local copies, waits for them, and re-layouts  4.3 us
  transfers between devices with their start and end apart: 2, of which 1 were waited for; matrix products, arithmetic and copies ran while one was open for 6% of the time, Pallas kernels for 0%

commit v1 on v0

--- a/solution.py
+++ b/solution.py
@@ -1,8 +1,11 @@
+import functools
 import math
 
 import jax
 import jax.numpy as jnp
 from jax import lax
+from jax.experimental import pallas as pl
+from jax.experimental.pallas import tpu as pltpu
 from jax.sharding import PartitionSpec as P
 
 FREQ = 256
@@ -114,6 +117,304 @@
     return (updated[None], velocity[None])
 
 
+MESH = pl.DeviceIdType.MESH
+ANY = pl.BlockSpec(memory_space=pl.ANY)
+VMEM = pl.BlockSpec(memory_space=pltpu.VMEM)
+
+
+def fused_kernel(
+    steps, seqs, stamps, latents, embed_hbm, mod_hbm, qkv_hbm, out_hbm,
+    updated, velocity,
+    lat_v, embed, mod_v, weight, out_v,
+    mod_part, mod_recv, mod_all, rows_all, lhs, fold_send, fold_recv,
+    vel_send, vel_recv, inc_send, inc_recv,
+    local_sem, a_send, a_get, b_send, b_get, x_send, x_get,
+    m_send, m_get, v_send, v_get, i_send, i_get,
+):
+    j, s = lax.axis_index("step"), lax.axis_index("seq")
+    rows, channels = lat_v.shape
+    width = embed.shape[1]
+    features = mod_hbm.shape[0]
+    block = mod_v.shape[1]
+    lanes = block // seqs
+    fold_rows = fold_recv.shape[1]
+    head_dim = out_v.shape[1]
+    half = features * seqs // 2
+
+    def seq_peer(i):
+        return lax.rem(s + i, seqs)
+
+    def step_peer(i):
+        return lax.rem(j + i, steps)
+
+    barrier = pltpu.get_barrier_semaphore()
+    for i in range(1, seqs):
+        pl.semaphore_signal(barrier, inc=1, device_id=(j, seq_peer(i)), device_id_type=MESH)
+    for i in range(1, steps):
+        pl.semaphore_signal(barrier, inc=1, device_id=(step_peer(i), s), device_id_type=MESH)
+
+    own_columns = pl.ds(pl.multiple_of(j * block, block), block)
+    loads = [
+        pltpu.make_async_copy(
+            mod_hbm.at[:, c, own_columns],
+            mod_v.at[pl.ds(c * features, features), :],
+            local_sem.at[c],
+        )
+        for c in range(2)
+    ]
+    load_lat = pltpu.make_async_copy(latents, lat_v, local_sem.at[2])
+    load_embed = pltpu.make_async_copy(embed_hbm, embed, local_sem.at[3])
+    load_weight = [
+        pltpu.make_async_copy(
+            qkv_hbm.at[c], weight.at[:, pl.ds(c * head_dim, head_dim)], local_sem.at[4 + c]
+        )
+        for c in range(3)
+    ]
+    load_out = pltpu.make_async_copy(out_hbm, out_v, local_sem.at[7])
+    for copy in (*loads, load_lat, load_embed, *load_weight, load_out):
+        copy.start()
+
+    shape = (2 * steps, 2 * features)
+    row = lax.broadcasted_iota(jnp.int32, shape, 0)
+    column = lax.broadcasted_iota(jnp.int32, shape, 1)
+    low_row, low_column = row < steps, column < features
+    step_of = jnp.where(low_row, row, row - steps)
+    feature = jnp.where(low_column, column, column - features) + s * features
+    is_cos = feature < half
+    index = jnp.where(is_cos, feature, feature - half)
+    stamp = jnp.zeros(shape, jnp.float32)
+    for k in range(steps):
+        stamp = jnp.where(step_of == k, stamps[k].astype(jnp.float32), stamp)
+    frequency = jnp.exp(-math.log(10000.0) * index.astype(jnp.float32) / half)
+    angle = stamp * frequency
+    condition = jnp.where(is_cos, jnp.cos(angle), jnp.sin(angle))
+    condition = jnp.where(low_row == low_column, condition, 0.0)
+
+    for copy in loads:
+        copy.wait()
+    part = jnp.dot(
+        condition, mod_v[...], precision=lax.Precision.HIGHEST, preferred_element_type=jnp.float32
+    )
+    for q in range(seqs):
+        mod_part[q] = part[:, q * lanes:(q + 1) * lanes]
+
+    pl.semaphore_wait(barrier, seqs + steps - 2)
+
+    def to_seq(i, src, dst, send, get):
+        return pltpu.make_async_remote_copy(
+            src_ref=src, dst_ref=dst, send_sem=send.at[i - 1], recv_sem=get.at[i - 1],
+            device_id=(j, seq_peer(i)), device_id_type=MESH,
+        )
+
+    def to_step(i, src, dst, send, get):
+        return pltpu.make_async_remote_copy(
+            src_ref=src, dst_ref=dst, send_sem=send.at[i - 1], recv_sem=get.at[i - 1],
+            device_id=(step_peer(i), s), device_id_type=MESH,
+        )
+
+    a_copies = [
+        to_seq(i, mod_part.at[seq_peer(i)], mod_recv.at[i - 1], a_send, a_get)
+        for i in range(1, seqs)
+    ]
+    for copy in a_copies:
+        copy.start()
+
+    load_lat.wait()
+    load_embed.wait()
+    own = lat_v[...].astype(jnp.bfloat16)
+    embedded = jnp.dot(own, embed[...], preferred_element_type=jnp.float32)
+    centered = embedded - jnp.mean(embedded, axis=-1, keepdims=True)
+    scale = lax.rsqrt(jnp.mean(centered * centered, axis=-1, keepdims=True) + 1e-06)
+    scale_high = scale.astype(jnp.bfloat16)
+    scale_low = (scale - scale_high.astype(jnp.float32)).astype(jnp.bfloat16)
+    rows_all[s] = jnp.concatenate(
+        [
+            own,
+            jnp.broadcast_to(scale_high, (rows, channels // 2)),
+            jnp.broadcast_to(scale_low, (rows, channels // 2)),
+        ],
+        axis=1,
+    )
+    x_copies = [
+        to_seq(i, rows_all.at[s], rows_all.at[s], x_send, x_get) for i in range(1, seqs)
+    ]
+    for copy in x_copies:
+        copy.start()
+
+    total = mod_part[s]
+    for i in range(1, seqs):
+        a_copies[i - 1].wait_recv()
+        total = total + mod_recv[i - 1]
+    mod_all[s] = total
+    b_copies = [
+        to_seq(i, mod_all.at[s], mod_all.at[s], b_send, b_get) for i in range(1, seqs)
+    ]
+    for copy in b_copies:
+        copy.start()
+
+    embed_mean = jnp.mean(embed[...].astype(jnp.float32), axis=-1, keepdims=True)
+    tail_row = lax.broadcasted_iota(jnp.int32, (fold_rows - channels, lanes), 0)
+    for copy in b_copies:
+        copy.wait_recv()
+    for q in range(seqs):
+        at = pl.ds(q * lanes, lanes)
+        own_at = pl.ds(pl.multiple_of(j * block + q * lanes, lanes), lanes)
+        embed_block = embed[:, own_at].astype(jnp.float32) - embed_mean
+        for i in range(steps):
+            k = step_peer(i)
+            shift_k = mod_all[q, pl.ds(k, 1), :]
+            scale_k = mod_all[q, pl.ds(steps + k, 1), :]
+            lhs[pl.ds(i * fold_rows, channels), at] = (embed_block * (1.0 + scale_k)).astype(
+                jnp.bfloat16
+            )
+            lhs[pl.ds(i * fold_rows + channels, fold_rows - channels), at] = jnp.where(
+                tail_row == 0, shift_k, 0.0
+            ).astype(jnp.bfloat16)
+
+    for copy in load_weight:
+        copy.wait()
+    folded = jnp.dot(lhs[...], weight[...], preferred_element_type=jnp.float32)
+    m_copies = []
+    for i in range(1, steps):
+        fold_send[i - 1] = folded[i * fold_rows:(i + 1) * fold_rows].astype(jnp.bfloat16)
+        copy = to_step(i, fold_send.at[i - 1], fold_recv.at[i - 1], m_send, m_get)
+        copy.start()
+        m_copies.append(copy)
+    for copy in x_copies:
+        copy.wait_recv()
+    tokens = rows_all[...].reshape(seqs * rows, 2 * channels)
+    latent_rows = tokens[:, :channels]
+    token_scale = tokens[:, channels:channels + 1].astype(jnp.float32) + tokens[
+        :, channels + channels // 2:channels + channels // 2 + 1
+    ].astype(jnp.float32)
+    matrix = folded[:fold_rows]
+    for i in range(1, steps):
+        m_copies[i - 1].wait_recv()
+        matrix = matrix + fold_recv[i - 1].astype(jnp.float32)
+    main = matrix[:channels]
+    main_high = main.astype(jnp.bfloat16)
+    main_low = (main - main_high.astype(jnp.float32)).astype(jnp.bfloat16)
+    projected = token_scale * (
+        jnp.dot(latent_rows, main_high, preferred_element_type=jnp.float32)
+        + jnp.dot(latent_rows, main_low, preferred_element_type=jnp.float32)
+    ) + matrix[channels:channels + 1]
+    projected = projected.astype(jnp.bfloat16)
+    queries = qk_norm(projected[:, :head_dim])
+    keys = qk_norm(projected[:, head_dim:2 * head_dim])
+    values = projected[:, 2 * head_dim:]
+    last = (((1,), (1,)), ((), ()))
+    scores = lax.dot_general(queries, keys, last, preferred_element_type=jnp.float32)
+    weights = jnp.exp(scores * (1.0 / math.sqrt(head_dim)))
+    probabilities = (weights / jnp.sum(weights, axis=-1, keepdims=True)).astype(jnp.bfloat16)
+    attended = jnp.dot(probabilities, values, preferred_element_type=jnp.float32).astype(
+        jnp.bfloat16
+    )
+    load_out.wait()
+    share = lax.dot_general(attended, out_v[...], last, preferred_element_type=jnp.float32)
+    for q in range(seqs):
+        vel_send[q] = share[q * rows:(q + 1) * rows]
+    v_copies = [
+        to_seq(i, vel_send.at[seq_peer(i)], vel_recv.at[i - 1], v_send, v_get)
+        for i in range(1, seqs)
+    ]
+    for copy in v_copies:
+        copy.start()
+    speed = vel_send[s]
+    for i in range(1, seqs):
+        v_copies[i - 1].wait_recv()
+        speed = speed + vel_recv[i - 1]
+    velocity[...] = speed
+
+    step_size = (stamps[j + 1].astype(jnp.float32) - stamps[j].astype(jnp.float32)) * 0.001
+    increment = step_size * speed + jnp.where(j == 0, lat_v[...], 0.0)
+    updated[...] = increment
+    inc_send[...] = increment
+    i_copies = [
+        to_step(i, inc_send, inc_recv.at[i - 1], i_send, i_get) for i in range(1, steps)
+    ]
+    for i in range(1, steps):
+        pl.when(j + i < steps)(i_copies[i - 1].start)
+    for i in range(1, steps):
+        @pl.when(j >= i)
+        def _():
+            i_copies[i - 1].wait_recv()
+            updated[...] += inc_recv[i - 1]
+
+    for copy in (*a_copies, *x_copies, *b_copies, *m_copies, *v_copies):
+        copy.wait_send()
+    for i in range(1, steps):
+        pl.when(j + i < steps)(i_copies[i - 1].wait_send)
+
+
+def fused(steps, seqs, latents, timesteps, embed_weight, mod_weight, qkv_weight, out_weight):
+    _, rows, channels = latents.shape
+    width = embed_weight.shape[1]
+    features = mod_weight.shape[0]
+    block, _, _, head_dim = qkv_weight.shape
+    lanes = block // seqs
+    fold_rows = channels + 16
+    bf16, f32 = jnp.bfloat16, jnp.float32
+    out_shape = jax.ShapeDtypeStruct((rows, channels), f32)
+    dma = pltpu.SemaphoreType.DMA
+    seq_sems = [dma((seqs - 1,))] * 2
+    step_sems = [dma((steps - 1,))] * 2
+    updated, velocity = pl.pallas_call(
+        functools.partial(fused_kernel, steps, seqs),
+        out_shape=(out_shape, out_shape),
+        in_specs=[pl.BlockSpec(memory_space=pltpu.SMEM)] + [ANY] * 5,
+        out_specs=(VMEM, VMEM),
+        scratch_shapes=[
+            pltpu.VMEM((rows, channels), f32),
+            pltpu.VMEM((channels, width), bf16),
+            pltpu.VMEM((2 * features, block), f32),
+            pltpu.VMEM((block, 3 * head_dim), bf16),
+            pltpu.VMEM((channels, head_dim), bf16),
+            pltpu.VMEM((seqs, 2 * steps, lanes), f32),
+            pltpu.VMEM((seqs - 1, 2 * steps, lanes), f32),
+            pltpu.VMEM((seqs, 2 * steps, lanes), f32),
+            pltpu.VMEM((seqs, rows, 2 * channels), bf16),
+            pltpu.VMEM((steps * fold_rows, block), bf16),
+            pltpu.VMEM((steps - 1, fold_rows, 3 * head_dim), bf16),
+            pltpu.VMEM((steps - 1, fold_rows, 3 * head_dim), bf16),
+            pltpu.VMEM((seqs, rows, channels), f32),
+            pltpu.VMEM((seqs - 1, rows, channels), f32),
+            pltpu.VMEM((rows, channels), f32),
+            pltpu.VMEM((steps - 1, rows, channels), f32),
+            dma((8,)),
+            *seq_sems, *seq_sems, *seq_sems, *step_sems, *seq_sems, *step_sems,
+        ],
+        compiler_params=pltpu.CompilerParams(
+            collective_id=0, has_side_effects=True, vmem_limit_bytes=32 * 1024 * 1024
+        ),
+    )(
+        timesteps,
+        latents[0],
+        embed_weight,
+        mod_weight,
+        jnp.transpose(qkv_weight, (1, 2, 0, 3))[0],
+        jnp.transpose(out_weight, (0, 2, 1))[0],
+    )
+    return updated[None], velocity[None]
+
+
+def body(steps, seqs, latents, timesteps, embed_weight, mod_weight, qkv_weight, out_weight):
+    block, heads_here, _, head_dim = qkv_weight.shape
+    fits = (
+        steps > 1
+        and seqs > 1
+        and latents.shape[0] == 1
+        and heads_here == 1
+        and steps % 4 == 0
+        and head_dim % 128 == 0
+        and block % (seqs * 128) == 0
+        and latents.shape[1] % 16 == 0
+        and latents.shape[2] % 16 == 0
+        and mod_weight.shape[0] % 8 == 0
+    )
+    run = functools.partial(fused, steps, seqs) if fits else on_device
+    return run(latents, timesteps, embed_weight, mod_weight, qkv_weight, out_weight)
+
+
 def solution(mesh):
     in_specs = (
         P("step", "seq", None),
@@ -125,5 +426,5 @@
     )
     out_specs = (P("step", "seq", None), P("step", "seq", None))
     return jax.shard_map(
-        on_device, mesh=mesh, in_specs=in_specs, out_specs=out_specs, check_vma=False
-    )
+        functools.partial(body, mesh.shape["step"], mesh.shape["seq"]), mesh=mesh, in_specs=in_specs, out_specs=out_specs, check_vma=False
+    )

time: 114 us -> 32.9 us (0.29)
  blocking collectives: 52.9 us -> 0 us
  waiting for transfers between devices: 27.3 us -> 0 us
  Pallas kernels: 0 us -> 25.2 us
  between operations: 15.4 us -> 0.65 us
  matrix products: 8.72 us -> 0 us
  other arithmetic: 4.22 us -> 0 us
  local copies, waits for them, and re-layouts: 5.06 us -> 6.69 us
    psum x1 -> x0, blocking collectives: 29.1 us -> none  [on_device(): modulation = lax.psum(partial_mod, 'seq')]
    reduce_scatter x1 -> x0, waiting for transfers between devices: 27.3 us -> none  [on_device(): lax.psum_scatter(jnp.dot(merged_heads, out_matrix, preferred_element_type...]
    pallas_call x0 -> x1, Pallas kernels: none -> 25.2 us  [fused(): pl.pallas_call(functools.partial(fused_kernel, steps, seqs), out_shape=(o...]
    all_gather x2 -> x0, blocking collectives: 23.8 us -> none  [the longest x1 15.7 us: on_device(): all_latents = lax.all_gather(own_latents, 'seq', axis=0, tiled=True)]
    dot_general x5 -> x0, matrix products: 8.72 us -> none  [the longest x1 4.48 us: on_device(): jnp.dot(gathered, flat_piece, preferred_element_type=jnp.float32)]
    unnamed x9 -> x14, local copies, waits for them, and re-layouts: 4.3 us -> 6.69 us
    convert_element_type x2 -> x0, other arithmetic: 1.45 us -> none  [the longest x1 0.73 us: on_device(): lax.dynamic_slice_in_dim(timesteps, step_index, 2, 0).astype(jnp.float32)]
  transfers between devices with their start and end apart: 2 -> 0, of which waited for: 1 -> 0; matrix products, arithmetic and copies ran while one was open for 6% -> 0% of each run, Pallas kernels for 0% -> 0%
where the time goes in v1:
time: 32.9 us; the launch traced here: 32.6 us
  Pallas kernels  25.2 us (77%)
  local copies, waits for them, and re-layouts  6.69 us (20%)
  between operations  0.65 us (2%)
    pallas_call x1, Pallas kernels, fused(): pl.pallas_call(functools.partial(fused_kernel, steps, seqs), out_shape=(o...  25.2 us
    unnamed x14, local copies, waits for them, and re-layouts  6.69 us

profile of v1, /device:TPU:0, one launch (start us, length us, event | category | flops | bytes accessed | tf_op | source)
XLA Modules:
  0.0 32.6 jit_solution(4134324414920596277)
XLA Ops:
  0.6 0.0 copy-start.5
  0.6 0.6 %copy-done.5 = s32[5]{0:T(128)S(1)} copy-done((s32[5]{0:T(128)S(1)}, s32[5]{0:T(128)}, u32[]{:S(2)}) %copy-start.5) | copy-done | bytes 44
  1.3 0.0 copy-start
  1.3 1.2 %copy-done = f32[32,2,4096]{2,1,0:T(2,128)S(1)} copy-done((f32[32,2,4096]{2,1,0:T(2,128)S(1)}, f32[32,2,4096]{2,1,0:T(2,128)}, u32[]{:S(2)}) %copy-start) | copy-done | bytes 1048600
  2.5 0.0 copy-start.1
  2.5 1.1 %copy-done.1 = bf16[1024,1,3,128]{3,0,2,1:T(8,128)(2,1)S(1)} copy-done((bf16[1024,1,3,128]{3,0,2,1:T(8,128)(2,1)S(1)}, bf16[1024,1,3,128]{3,0,2,1:T(8,128)(2,1)}, u32[]{:S(2)}) %copy-start.1) | copy-done | bytes 786456
  3.6 0.0 copy-start.2
  3.6 1.0 %copy-done.2 = bf16[64,4096]{1,0:T(8,128)(2,1)S(1)} copy-done((bf16[64,4096]{1,0:T(8,128)(2,1)S(1)}, bf16[64,4096]{1,0:T(8,128)(2,1)}, u32[]{:S(2)}) %copy-start.2) | copy-done | bytes 524312
  4.7 0.0 copy-start.3
  4.7 0.7 %copy-done.3 = f32[1,32,64]{2,1,0:T(8,128)S(1)} copy-done((f32[1,32,64]{2,1,0:T(8,128)S(1)}, f32[1,32,64]{2,1,0:T(8,128)}, u32[]{:S(2)}) %copy-start.3) | copy-done | bytes 8216
  5.4 0.0 copy-start.4
  5.4 0.7 %copy-done.4 = bf16[1,128,64]{1,2,0:T(8,128)(2,1)S(1)} copy-done((bf16[1,128,64]{1,2,0:T(8,128)(2,1)S(1)}, bf16[1,128,64]{1,2,0:T(8,128)(2,1)}, u32[]{:S(2)}) %copy-start.4) | copy-done | bytes 16408
  6.1 25.2 %shard_map.77 = (f32[32,64]{1,0:T(8,128)S(1)}, f32[32,64]{1,0:T(8,128)S(1)}) custom-call(s32[5]{0:T(128)S(1)} %copy-done.5, f32[32,64]{1,0:T(8,128)S(1)} %bitcast.10, bf16[64,4096]{1,0:T(8,128)(2,1)S(1)} %copy-done.2, f32[32,2,4096]{2,1,0:T(2,128)S(1)} %copy-done, bf16[3,1024,128]{2,1,0:T(8,128)(2,1)S(1)} %bitcast.9, bf16[64,128]{1,0:T(8,128)(2,1)S(1)} %bitcast.11), custom_call_target="tpu_custom_call" | custom-call | tf_op jit(solution)/shard_map/pallas_call | solution.py:361
  31.4 0.6 %copy.10 = f32[1,32,64]{2,1,0:T(8,128)} copy(f32[1,32,64]{2,1,0:T(8,128)S(1)} %bitcast.13) | data formatting | bytes 16384
  32.0 0.6 %copy.11 = f32[1,32,64]{2,1,0:T(8,128)} copy(f32[1,32,64]{2,1,0:T(8,128)S(1)} %bitcast.12) | data formatting | bytes 16384
Async XLA Ops:
  0.6 0.7 %copy-start.5 = (s32[5]{0:T(128)S(1)}, s32[5]{0:T(128)}, u32[]{:S(2)}) copy-start(s32[5]{0:T(128)} %stamps.1) | copy-start | bytes 64
  1.3 1.2 %copy-start = (f32[32,2,4096]{2,1,0:T(2,128)S(1)}, f32[32,2,4096]{2,1,0:T(2,128)}, u32[]{:S(2)}) copy-start(f32[32,2,4096]{2,1,0:T(2,128)} %mod_hbm.1) | copy-start | bytes 3145732
  2.5 1.1 %copy-start.1 = (bf16[1024,1,3,128]{3,0,2,1:T(8,128)(2,1)S(1)}, bf16[1024,1,3,128]{3,0,2,1:T(8,128)(2,1)}, u32[]{:S(2)}) copy-start(bf16[1024,1,3,128]{3,0,2,1:T(8,128)(2,1)} %param.10) | copy-start | bytes 2359300
  3.6 1.0 %copy-start.2 = (bf16[64,4096]{1,0:T(8,128)(2,1)S(1)}, bf16[64,4096]{1,0:T(8,128)(2,1)}, u32[]{:S(2)}) copy-start(bf16[64,4096]{1,0:T(8,128)(2,1)} %embed_hbm.1) | copy-start | bytes 1572868
  4.7 0.7 %copy-start.3 = (f32[1,32,64]{2,1,0:T(8,128)S(1)}, f32[1,32,64]{2,1,0:T(8,128)}, u32[]{:S(2)}) copy-start(f32[1,32,64]{2,1,0:T(8,128)} %param.6) | copy-start | bytes 24580
  5.4 0.7 %copy-start.4 = (bf16[1,128,64]{1,2,0:T(8,128)(2,1)S(1)}, bf16[1,128,64]{1,2,0:T(8,128)(2,1)}, u32[]{:S(2)}) copy-start(bf16[1,128,64]{1,2,0:T(8,128)(2,1)} %param.11) | copy-start | bytes 49156

commit v2 on v1

--- a/solution.py
+++ b/solution.py
@@ -118,15 +118,15 @@
 
 
 MESH = pl.DeviceIdType.MESH
-ANY = pl.BlockSpec(memory_space=pl.ANY)
+HBM = pl.BlockSpec(memory_space=pltpu.HBM)
 VMEM = pl.BlockSpec(memory_space=pltpu.VMEM)
 
 
 def fused_kernel(
     steps, seqs, stamps, latents, embed_hbm, mod_hbm, qkv_hbm, out_hbm,
-    updated, velocity,
+    result,
     lat_v, embed, mod_v, weight, out_v,
-    mod_part, mod_recv, mod_all, rows_all, lhs, fold_send, fold_recv,
+    mod_part, mod_recv, mod_all, rows_all, embed_own, lhs, fold_send, fold_recv,
     vel_send, vel_recv, inc_send, inc_recv,
     local_sem, a_send, a_get, b_send, b_get, x_send, x_get,
     m_send, m_get, v_send, v_get, i_send, i_get,
@@ -253,13 +253,13 @@
         copy.start()
 
     embed_mean = jnp.mean(embed[...].astype(jnp.float32), axis=-1, keepdims=True)
+    embed_own[...] = embed[:, own_columns].astype(jnp.float32) - embed_mean
     tail_row = lax.broadcasted_iota(jnp.int32, (fold_rows - channels, lanes), 0)
     for copy in b_copies:
         copy.wait_recv()
     for q in range(seqs):
         at = pl.ds(q * lanes, lanes)
-        own_at = pl.ds(pl.multiple_of(j * block + q * lanes, lanes), lanes)
-        embed_block = embed[:, own_at].astype(jnp.float32) - embed_mean
+        embed_block = embed_own[:, at]
         for i in range(steps):
             k = step_peer(i)
             shift_k = mod_all[q, pl.ds(k, 1), :]
@@ -323,11 +323,11 @@
     for i in range(1, seqs):
         v_copies[i - 1].wait_recv()
         speed = speed + vel_recv[i - 1]
-    velocity[...] = speed
+    result[:, channels:] = speed
 
     step_size = (stamps[j + 1].astype(jnp.float32) - stamps[j].astype(jnp.float32)) * 0.001
     increment = step_size * speed + jnp.where(j == 0, lat_v[...], 0.0)
-    updated[...] = increment
+    result[:, :channels] = increment
     inc_send[...] = increment
     i_copies = [
         to_step(i, inc_send, inc_recv.at[i - 1], i_send, i_get) for i in range(1, steps)
@@ -338,7 +338,7 @@
         @pl.when(j >= i)
         def _():
             i_copies[i - 1].wait_recv()
-            updated[...] += inc_recv[i - 1]
+            result[:, :channels] += inc_recv[i - 1]
 
     for copy in (*a_copies, *x_copies, *b_copies, *m_copies, *v_copies):
         copy.wait_send()
@@ -354,15 +354,15 @@
     lanes = block // seqs
     fold_rows = channels + 16
     bf16, f32 = jnp.bfloat16, jnp.float32
-    out_shape = jax.ShapeDtypeStruct((rows, channels), f32)
+    out_shape = jax.ShapeDtypeStruct((rows, 2 * channels), f32)
     dma = pltpu.SemaphoreType.DMA
     seq_sems = [dma((seqs - 1,))] * 2
     step_sems = [dma((steps - 1,))] * 2
-    updated, velocity = pl.pallas_call(
+    result = pl.pallas_call(
         functools.partial(fused_kernel, steps, seqs),
-        out_shape=(out_shape, out_shape),
-        in_specs=[pl.BlockSpec(memory_space=pltpu.SMEM)] + [ANY] * 5,
-        out_specs=(VMEM, VMEM),
+        out_shape=out_shape,
+        in_specs=[pl.BlockSpec(memory_space=pltpu.SMEM)] + [HBM] * 5,
+        out_specs=VMEM,
         scratch_shapes=[
             pltpu.VMEM((rows, channels), f32),
             pltpu.VMEM((channels, width), bf16),
@@ -373,6 +373,7 @@
             pltpu.VMEM((seqs - 1, 2 * steps, lanes), f32),
             pltpu.VMEM((seqs, 2 * steps, lanes), f32),
             pltpu.VMEM((seqs, rows, 2 * channels), bf16),
+            pltpu.VMEM((channels, block), f32),
             pltpu.VMEM((steps * fold_rows, block), bf16),
             pltpu.VMEM((steps - 1, fold_rows, 3 * head_dim), bf16),
             pltpu.VMEM((steps - 1, fold_rows, 3 * head_dim), bf16),
@@ -384,7 +385,7 @@
             *seq_sems, *seq_sems, *seq_sems, *step_sems, *seq_sems, *step_sems,
         ],
         compiler_params=pltpu.CompilerParams(
-            collective_id=0, has_side_effects=True, vmem_limit_bytes=32 * 1024 * 1024
+            collective_id=0, has_side_effects=True, vmem_limit_bytes=56 * 1024 * 1024
         ),
     )(
         timesteps,
@@ -394,7 +395,7 @@
         jnp.transpose(qkv_weight, (1, 2, 0, 3))[0],
         jnp.transpose(out_weight, (0, 2, 1))[0],
     )
-    return updated[None], velocity[None]
+    return result[None, :, :channels], result[None, :, channels:]
 
 
 def body(steps, seqs, latents, timesteps, embed_weight, mod_weight, qkv_weight, out_weight):

time: 32.9 us -> 28.4 us (0.86)
  local copies, waits for them, and re-layouts: 6.69 us -> 1.47 us
  Pallas kernels: 25.2 us -> 25.9 us
    unnamed x14 -> x0, local copies, waits for them, and re-layouts: 6.69 us -> none
    broadcast_in_dim x0 -> x1, local copies, waits for them, and re-layouts: none -> 1.47 us  [fused(): return (result[None, :, :channels], result[None, :, channels:])]
    pallas_call x1, Pallas kernels: 25.2 us -> 25.9 us  [fused(): pl.pallas_call(functools.partial(fused_kernel, steps, seqs), out_shape=ou...]
where the time goes in v2:
time: 28.4 us; the launch traced here: 28 us
  Pallas kernels  25.9 us (91%)
  local copies, waits for them, and re-layouts  1.47 us (5%)
  between operations  0.64 us (2%)
    pallas_call x1, Pallas kernels, fused(): pl.pallas_call(functools.partial(fused_kernel, steps, seqs), out_shape=ou...  25.9 us
    broadcast_in_dim x1, local copies, waits for them, and re-layouts, fused(): return (result[None, :, :channels], result[None, :, channels:])  1.47 us

profile of v2, /device:TPU:0, one launch (start us, length us, event | category | flops | bytes accessed | tf_op | source)
XLA Modules:
  0.0 28.0 jit_solution(16717220707222580280)
XLA Ops:
  0.6 25.9 %shard_map.77 = f32[32,128]{1,0:T(8,128)} custom-call(s32[5]{0:T(128)} %stamps.1, f32[32,64]{1,0:T(8,128)} %bitcast.12, bf16[64,4096]{1,0:T(8,128)(2,1)} %embed_hbm.1, f32[32,2,4096]{2,1,0:T(2,128)} %mod_hbm.1, bf16[3,1024,128]{2,1,0:T(8,128)(2,1)} %bitcast.11, bf16[64,128]{1,0:T(8,128)(2,1)} %bitcast.13), custom_call_target="tpu_custom_call" | custom-call | tf_op jit(solution)/shard_map/pallas_call | solution.py:361
  26.5 1.5 %slice_bitcast_fusion = (f32[1,32,64]{2,1,0:T(8,128)}, f32[1,32,64]{2,1,0:T(8,128)}) fusion(f32[32,128]{1,0:T(8,128)} %shard_map.77), kind=kLoop, calls=%fused_computation | loop fusion | bytes 32768 | tf_op jit(solution)/shard_map/broadcast_in_dim | solution.py:398

commit v3 on v2

--- a/solution.py
+++ b/solution.py
@@ -235,11 +235,6 @@
         ],
         axis=1,
     )
-    x_copies = [
-        to_seq(i, rows_all.at[s], rows_all.at[s], x_send, x_get) for i in range(1, seqs)
-    ]
-    for copy in x_copies:
-        copy.start()
 
     total = mod_part[s]
     for i in range(1, seqs):
@@ -251,35 +246,44 @@
     ]
     for copy in b_copies:
         copy.start()
+    x_copies = [
+        to_seq(i, rows_all.at[s], rows_all.at[s], x_send, x_get) for i in range(1, seqs)
+    ]
+    for copy in x_copies:
+        copy.start()
 
     embed_mean = jnp.mean(embed[...].astype(jnp.float32), axis=-1, keepdims=True)
     embed_own[...] = embed[:, own_columns].astype(jnp.float32) - embed_mean
     tail_row = lax.broadcasted_iota(jnp.int32, (fold_rows - channels, lanes), 0)
     for copy in b_copies:
         copy.wait_recv()
-    for q in range(seqs):
-        at = pl.ds(q * lanes, lanes)
-        embed_block = embed_own[:, at]
-        for i in range(steps):
-            k = step_peer(i)
+    for copy in load_weight:
+        copy.wait()
+
+    def fold(i):
+        k = step_peer(i)
+        for q in range(seqs):
+            at = pl.ds(q * lanes, lanes)
             shift_k = mod_all[q, pl.ds(k, 1), :]
             scale_k = mod_all[q, pl.ds(steps + k, 1), :]
-            lhs[pl.ds(i * fold_rows, channels), at] = (embed_block * (1.0 + scale_k)).astype(
-                jnp.bfloat16
-            )
+            lhs[pl.ds(i * fold_rows, channels), at] = (
+                embed_own[:, at] * (1.0 + scale_k)
+            ).astype(jnp.bfloat16)
             lhs[pl.ds(i * fold_rows + channels, fold_rows - channels), at] = jnp.where(
                 tail_row == 0, shift_k, 0.0
             ).astype(jnp.bfloat16)
-
-    for copy in load_weight:
-        copy.wait()
-    folded = jnp.dot(lhs[...], weight[...], preferred_element_type=jnp.float32)
+        return jnp.dot(
+            lhs[pl.ds(i * fold_rows, fold_rows), :], weight[...],
+            preferred_element_type=jnp.float32,
+        )
+
     m_copies = []
     for i in range(1, steps):
-        fold_send[i - 1] = folded[i * fold_rows:(i + 1) * fold_rows].astype(jnp.bfloat16)
+        fold_send[i - 1] = fold(i).astype(jnp.bfloat16)
         copy = to_step(i, fold_send.at[i - 1], fold_recv.at[i - 1], m_send, m_get)
         copy.start()
         m_copies.append(copy)
+    matrix = fold(0)
     for copy in x_copies:
         copy.wait_recv()
     tokens = rows_all[...].reshape(seqs * rows, 2 * channels)
@@ -287,7 +291,6 @@
     token_scale = tokens[:, channels:channels + 1].astype(jnp.float32) + tokens[
         :, channels + channels // 2:channels + channels // 2 + 1
     ].astype(jnp.float32)
-    matrix = folded[:fold_rows]
     for i in range(1, steps):
         m_copies[i - 1].wait_recv()
         matrix = matrix + fold_recv[i - 1].astype(jnp.float32)
@@ -360,7 +363,7 @@
     step_sems = [dma((steps - 1,))] * 2
     result = pl.pallas_call(
         functools.partial(fused_kernel, steps, seqs),
-        out_shape=out_shape,
+        out_shape=pltpu.VMEM((rows, 2 * channels), f32),
         in_specs=[pl.BlockSpec(memory_space=pltpu.SMEM)] + [HBM] * 5,
         out_specs=VMEM,
         scratch_shapes=[

time: 28.4 us -> 26.9 us (0.947)
  local copies, waits for them, and re-layouts: 1.47 us -> 0.68 us
  Pallas kernels: 25.9 us -> 25.4 us
    broadcast_in_dim x1, local copies, waits for them, and re-layouts: 1.47 us -> 0.68 us  [fused(): return (result[None, :, :channels], result[None, :, channels:])]
    pallas_call x1, Pallas kernels: 25.9 us -> 25.4 us  [fused(): pl.pallas_call(functools.partial(fused_kernel, steps, seqs), out_shape=pl...]
where the time goes in v3:
time: 26.9 us; the launch traced here: 26.7 us
  Pallas kernels  25.4 us (94%)
  local copies, waits for them, and re-layouts  0.68 us (3%)
  between operations  0.64 us (2%)
    pallas_call x1, Pallas kernels, fused(): pl.pallas_call(functools.partial(fused_kernel, steps, seqs), out_shape=pl...  25.4 us
    broadcast_in_dim x1, local copies, waits for them, and re-layouts, fused(): return (result[None, :, :channels], result[None, :, channels:])  0.68 us

profile of v3, /device:TPU:0, one launch (start us, length us, event | category | flops | bytes accessed | tf_op | source)
XLA Modules:
  0.0 26.7 jit_solution(7729501264167386081)
XLA Ops:
  0.6 25.4 %shard_map.77 = f32[32,128]{1,0:T(8,128)S(1)} custom-call(s32[5]{0:T(128)} %stamps.1, f32[32,64]{1,0:T(8,128)} %bitcast.12, bf16[64,4096]{1,0:T(8,128)(2,1)} %embed_hbm.1, f32[32,2,4096]{2,1,0:T(2,128)} %mod_hbm.1, bf16[3,1024,128]{2,1,0:T(8,128)(2,1)} %bitcast.11, bf16[64,128]{1,0:T(8,128)(2,1)} %bitcast.13), custom_call_target="tpu_custom_call" | custom-call | tf_op jit(solution)/shard_map/pallas_call | solution.py:364
  26.0 0.7 %slice_bitcast_fusion = (f32[1,32,64]{2,1,0:T(8,128)}, f32[1,32,64]{2,1,0:T(8,128)}) fusion(f32[32,128]{1,0:T(8,128)S(1)} %shard_map.77), kind=kLoop, calls=%fused_computation | loop fusion | bytes 32768 | tf_op jit(solution)/shard_map/broadcast_in_dim | solution.py:401

commit v4 on v3

--- a/solution.py
+++ b/solution.py
@@ -123,9 +123,9 @@
 
 
 def fused_kernel(
-    steps, seqs, stamps, latents, embed_hbm, mod_hbm, qkv_hbm, out_hbm,
+    steps, seqs, stamps_hbm, latents, embed_hbm, mod_hbm, qkv_hbm, out_hbm,
     result,
-    lat_v, embed, mod_v, weight, out_v,
+    stamps, lat_v, embed, mod_v, weight, out_v,
     mod_part, mod_recv, mod_all, rows_all, embed_own, lhs, fold_send, fold_recv,
     vel_send, vel_recv, inc_send, inc_recv,
     local_sem, a_send, a_get, b_send, b_get, x_send, x_get,
@@ -170,8 +170,9 @@
         )
         for c in range(3)
     ]
+    load_stamps = pltpu.make_async_copy(stamps_hbm, stamps, local_sem.at[8])
     load_out = pltpu.make_async_copy(out_hbm, out_v, local_sem.at[7])
-    for copy in (*loads, load_lat, load_embed, *load_weight, load_out):
+    for copy in (load_stamps, *loads, load_lat, load_embed, *load_weight, load_out):
         copy.start()
 
     shape = (2 * steps, 2 * features)
@@ -183,6 +184,7 @@
     is_cos = feature < half
     index = jnp.where(is_cos, feature, feature - half)
     stamp = jnp.zeros(shape, jnp.float32)
+    load_stamps.wait()
     for k in range(steps):
         stamp = jnp.where(step_of == k, stamps[k].astype(jnp.float32), stamp)
     frequency = jnp.exp(-math.log(10000.0) * index.astype(jnp.float32) / half)
@@ -364,9 +366,10 @@
     result = pl.pallas_call(
         functools.partial(fused_kernel, steps, seqs),
         out_shape=pltpu.VMEM((rows, 2 * channels), f32),
-        in_specs=[pl.BlockSpec(memory_space=pltpu.SMEM)] + [HBM] * 5,
+        in_specs=[HBM] * 6,
         out_specs=VMEM,
         scratch_shapes=[
+            pltpu.SMEM(timesteps.shape, jnp.int32),
             pltpu.VMEM((rows, channels), f32),
             pltpu.VMEM((channels, width), bf16),
             pltpu.VMEM((2 * features, block), f32),
@@ -384,7 +387,7 @@
             pltpu.VMEM((seqs - 1, rows, channels), f32),
             pltpu.VMEM((rows, channels), f32),
             pltpu.VMEM((steps - 1, rows, channels), f32),
-            dma((8,)),
+            dma((9,)),
             *seq_sems, *seq_sems, *seq_sems, *step_sems, *seq_sems, *step_sems,
         ],
         compiler_params=pltpu.CompilerParams(

time: 26.9 us -> 26.2 us (0.974)
  Pallas kernels: 25.4 us -> 24.7 us
    pallas_call x1, Pallas kernels: 25.4 us -> 24.7 us  [fused(): pl.pallas_call(functools.partial(fused_kernel, steps, seqs), out_shape=pl...]
where the time goes in v4:
time: 26.2 us; the launch traced here: 26.1 us
  Pallas kernels  24.7 us (94%)
  local copies, waits for them, and re-layouts  0.68 us (3%)
  between operations  0.64 us (2%)
    pallas_call x1, Pallas kernels, fused(): pl.pallas_call(functools.partial(fused_kernel, steps, seqs), out_shape=pl...  24.7 us
    broadcast_in_dim x1, local copies, waits for them, and re-layouts, fused(): return (result[None, :, :channels], result[None, :, channels:])  0.68 us

profile of v4, /device:TPU:0, one launch (start us, length us, event | category | flops | bytes accessed | tf_op | source)
XLA Modules:
  0.0 26.1 jit_solution(17188529282306516584)
XLA Ops:
  0.6 24.7 %shard_map.77 = f32[32,128]{1,0:T(8,128)S(1)} custom-call(s32[5]{0:T(128)} %stamps_hbm.1, f32[32,64]{1,0:T(8,128)} %bitcast.12, bf16[64,4096]{1,0:T(8,128)(2,1)} %embed_hbm.1, f32[32,2,4096]{2,1,0:T(2,128)} %mod_hbm.1, bf16[3,1024,128]{2,1,0:T(8,128)(2,1)} %bitcast.11, bf16[64,128]{1,0:T(8,128)(2,1)} %bitcast.13), custom_call_target="tpu_custom_call" | custom-call | tf_op jit(solution)/shard_map/pallas_call | solution.py:366
  25.4 0.7 %slice_bitcast_fusion = (f32[1,32,64]{2,1,0:T(8,128)}, f32[1,32,64]{2,1,0:T(8,128)}) fusion(f32[32,128]{1,0:T(8,128)S(1)} %shard_map.77), kind=kLoop, calls=%fused_computation | loop fusion | bytes 32768 | tf_op jit(solution)/shard_map/broadcast_in_dim | solution.py:404
